TPU v7x, 32 devices: a whole 2x2x4 slice. The times are simulated.
32 devices in a mesh: dp: 8 (over y, x, core), tensor: 4 (over z).
Axes of the slice: x: 2, y: 2, z: 4, core: 2. Of those that a mesh axis runs over, the one named last changes fastest.
Arguments:
- inputs: bfloat16 [8192, 1024], P('dp', 'tensor'), may hold values from -6 to 6
- lengths: int32 [8], P('dp'), may hold values from 512 to 1024, as said below
- random_blocks: int32 [8, 16, 16, 3], P('dp', 'tensor'), may hold values from 1 to 14
- attn_norm_gain: bfloat16 [1024], P('tensor'), may hold values from 0.5 to 1.5
- attn_norm_bias: bfloat16 [1024], P('tensor'), may hold values from -1.75 to 1.75
- query_weight: bfloat16 [1024, 1024], P(None, 'tensor'), may hold values from -0.1875 to 0.1875
- query_bias: bfloat16 [1024], P('tensor'), may hold values from -1.75 to 1.75
- key_weight: bfloat16 [1024, 1024], P(None, 'tensor'), may hold values from -0.1875 to 0.1875
- value_weight: bfloat16 [1024, 1024], P(None, 'tensor'), may hold values from -0.1875 to 0.1875
- value_bias: bfloat16 [1024], P('tensor'), may hold values from -1.75 to 1.75
- out_weight: bfloat16 [1024, 1024], P('tensor'), may hold values from -2 to 2
- out_bias: bfloat16 [1024], P('tensor'), may hold values from -1.75 to 1.75
- ffn_norm_gain: bfloat16 [1024], P('tensor'), may hold values from 0.2 to 2.2
- ffn_norm_bias: bfloat16 [1024], P('tensor'), may hold values from -1.75 to 1.75
- up_weight: bfloat16 [1024, 4096], P(None, 'tensor'), may hold values from -1 to 1
- up_bias: bfloat16 [4096], P('tensor'), may hold values from -1.75 to 1.75
- down_weight: bfloat16 [4096, 1024], P('tensor'), may hold values from -0.09375 to 0.09375
- down_bias: bfloat16 [1024], P('tensor'), may hold values from -1.75 to 1.75
- grad_out: bfloat16 [8192, 1024], P('dp', 'tensor'), may hold values from -6 to 6
Outputs:
- outputs: bfloat16 [8192, 1024], P('dp', 'tensor')
- grad_inputs: bfloat16 [8192, 1024], P('dp', 'tensor')
- grad_attn_norm_gain: float32 [1024], P('tensor')
- grad_attn_norm_bias: float32 [1024], P('tensor')
- grad_query_weight: float32 [1024, 1024], P(None, 'tensor')
- grad_query_bias: float32 [1024], P('tensor')
- grad_key_weight: float32 [1024, 1024], P(None, 'tensor')
- grad_value_weight: float32 [1024, 1024], P(None, 'tensor')
- grad_value_bias: float32 [1024], P('tensor')
- grad_out_weight: float32 [1024, 1024], P('tensor')
- grad_out_bias: float32 [1024], P('tensor')
- grad_ffn_norm_gain: float32 [1024], P('tensor')
- grad_ffn_norm_bias: float32 [1024], P('tensor')
- grad_up_weight: float32 [1024, 4096], P(None, 'tensor')
- grad_up_bias: float32 [4096], P('tensor')
- grad_down_weight: float32 [4096, 1024], P('tensor')
- grad_down_bias: float32 [1024], P('tensor')
Inputs may be any that keep to these rules, and one draw needn't show every extreme that they name: `lengths`: valid tokens of each sequence; some sequence has exactly 1024.
All inputs are finite; a program needn't handle non-finite values.
Results may differ from a plain program's by a relative error of at most 0.018.
Values may be sent and summed in bfloat16 or wider, within the bound.
No kernel may reach another device: no remote copies, remote signals or barrier semaphores. Data moves between devices by JAX's collectives and lax.ppermute only.
A program may use at most 128 MiB of HBM per device.

v0:
```python
from functools import partial

import jax
import jax.numpy as jnp
from jax import lax
from jax.sharding import PartitionSpec as P

D = 1024
HD = 64
BLOCK = 64
LEN = 1024
NB = 16
QB = 512


eps_norm = 1e-05


def normalize(values):
    average = jnp.mean(values, axis=-1, keepdims=True)
    centered = values - average
    inv_std = lax.rsqrt(jnp.mean(centered * centered, axis=-1, keepdims=True) + eps_norm)
    return (centered * inv_std, inv_std)


def block_allowed(random_rows):
    row_ids = jnp.arange(NB, dtype=jnp.int32)[:, None]
    col_ids = jnp.arange(NB, dtype=jnp.int32)[None, :]
    fixed_part = (
        (row_ids == 0)
        | (row_ids == NB - 1)
        | (col_ids == 0)
        | (col_ids == NB - 1)
        | (jnp.abs(row_ids - col_ids) <= 1)
    )
    chosen = jnp.any(
        random_rows[:, :, :, None] == jnp.arange(NB, dtype=jnp.int32)[None, None, None, :], axis=2
    )
    return fixed_part[None] | chosen


def tile_mask(allowed_blocks, key_valid, tile_id):
    tile_blocks = lax.dynamic_slice_in_dim(allowed_blocks, tile_id * (QB // BLOCK), QB // BLOCK, 1)
    expanded = jnp.repeat(jnp.repeat(tile_blocks, BLOCK, axis=1), BLOCK, axis=2)
    return expanded & key_valid[None, None, :]


def attend_forward(queries, key_rows, val_rows, allowed_blocks, key_valid):

    def tile_fn(tile_id):
        tile_q = lax.dynamic_slice_in_dim(queries, tile_id * QB, QB, 0)
        scores = (
            jnp.einsum("qhd,khd->hqk", tile_q, key_rows, preferred_element_type=jnp.float32) * 0.125
        )
        scores = jnp.where(tile_mask(allowed_blocks, key_valid, tile_id), scores, -1e30)
        row_top = jnp.max(scores, axis=-1, keepdims=True)
        raised = jnp.exp(scores - row_top)
        row_total = jnp.sum(raised, axis=-1, keepdims=True)
        prob_low = (raised / row_total).astype(jnp.bfloat16)
        context = jnp.einsum("hqk,khd->qhd", prob_low, val_rows, preferred_element_type=jnp.float32)
        return (context.astype(jnp.bfloat16), (row_top + jnp.log(row_total))[..., 0])

    contexts, log_totals = lax.map(tile_fn, jnp.arange(LEN // QB, dtype=jnp.int32))
    return (contexts.reshape(LEN, -1), log_totals)


def attend_backward(
    queries, key_rows, val_rows, grad_context, log_totals, allowed_blocks, key_valid
):

    def tile_step(carry, tile_id):
        grad_keys, grad_vals = carry
        tile_q = lax.dynamic_slice_in_dim(queries, tile_id * QB, QB, 0)
        tile_grad = lax.dynamic_slice_in_dim(grad_context, tile_id * QB, QB, 0)
        scores = (
            jnp.einsum("qhd,khd->hqk", tile_q, key_rows, preferred_element_type=jnp.float32) * 0.125
        )
        allowed = tile_mask(allowed_blocks, key_valid, tile_id)
        attn_prob = jnp.where(allowed, jnp.exp(scores - log_totals[tile_id][:, :, None]), 0.0)
        prob_low = attn_prob.astype(jnp.bfloat16)
        grad_prob = jnp.einsum(
            "qhd,khd->hqk", tile_grad, val_rows, preferred_element_type=jnp.float32
        )
        inner = jnp.sum(attn_prob * grad_prob, axis=-1, keepdims=True)
        grad_scores = (attn_prob * (grad_prob - inner)).astype(jnp.bfloat16)
        grad_q = (
            jnp.einsum("hqk,khd->qhd", grad_scores, key_rows, preferred_element_type=jnp.float32)
            * 0.125
        )
        grad_keys = (
            grad_keys
            + jnp.einsum("hqk,qhd->khd", grad_scores, tile_q, preferred_element_type=jnp.float32)
            * 0.125
        )
        grad_vals = grad_vals + jnp.einsum(
            "hqk,qhd->khd", prob_low, tile_grad, preferred_element_type=jnp.float32
        )
        return ((grad_keys, grad_vals), grad_q)

    zeros_init = jnp.zeros(key_rows.shape, jnp.float32)
    (grad_keys, grad_vals), grad_qs = lax.scan(
        tile_step, (zeros_init, zeros_init), jnp.arange(LEN // QB, dtype=jnp.int32)
    )
    return (grad_qs.reshape(LEN, -1), grad_keys.reshape(LEN, -1), grad_vals.reshape(LEN, -1))


def shards(
    inputs,
    lengths,
    random_blocks,
    attn_norm_gain,
    attn_norm_bias,
    query_weight,
    query_bias,
    key_weight,
    value_weight,
    value_bias,
    out_weight,
    out_bias,
    ffn_norm_gain,
    ffn_norm_bias,
    up_weight,
    up_bias,
    down_weight,
    down_bias,
    grad_out,
):
    f32 = jnp.float32
    bf16 = jnp.bfloat16
    width_local = inputs.shape[1]
    token_count = inputs.shape[0]
    seq_count = token_count // LEN
    col_start = lax.axis_index("tensor") * width_local
    small_local = jnp.stack(
        [attn_norm_gain, attn_norm_bias, out_bias, ffn_norm_gain, ffn_norm_bias, down_bias]
    )
    full_inputs, small_full = (
        lax.all_gather(inputs, "tensor", axis=1, tiled=True),
        lax.all_gather(small_local, "tensor", axis=1, tiled=True),
    )
    small_values = small_full.astype(f32)
    gain_one = small_values[0]
    bias_one = small_values[1]
    out_shift = small_values[2]
    gain_two = small_values[3]
    bias_two = small_values[4]
    inputs_f = full_inputs.astype(f32)
    unit_one, inv_one = normalize(inputs_f)
    normed_one = (unit_one * gain_one + bias_one).astype(bf16)
    queries = (
        jnp.dot(normed_one, query_weight, preferred_element_type=f32) + query_bias.astype(f32)
    ).astype(bf16)
    key_rows = jnp.dot(normed_one, key_weight, preferred_element_type=f32).astype(bf16)
    val_rows = (
        jnp.dot(normed_one, value_weight, preferred_element_type=f32) + value_bias.astype(f32)
    ).astype(bf16)
    heads_local = query_weight.shape[1] // HD
    query_heads = queries.reshape(seq_count, LEN, heads_local, HD)
    key_heads = key_rows.reshape(seq_count, LEN, heads_local, HD)
    val_heads = val_rows.reshape(seq_count, LEN, heads_local, HD)
    position = jnp.arange(LEN, dtype=jnp.int32)
    seq_id = 0
    allowed_blocks = block_allowed(random_blocks[seq_id])
    key_valid = position < lengths[seq_id]
    masks_kept = [(allowed_blocks, key_valid)]
    seq_context, seq_totals = attend_forward(
        query_heads[seq_id], key_heads[seq_id], val_heads[seq_id], allowed_blocks, key_valid
    )
    totals_kept = [seq_totals]
    attn_part = jnp.dot(seq_context, out_weight, preferred_element_type=f32)
    attn_full = lax.psum(attn_part, "tensor")
    resid_full = inputs_f + attn_full + out_shift
    resid_local = lax.dynamic_slice_in_dim(resid_full, col_start, width_local, 1)
    unit_two, inv_two = normalize(resid_full)
    normed_two = (unit_two * gain_two + bias_two).astype(bf16)
    up_proj = jnp.dot(normed_two, up_weight, preferred_element_type=f32) + up_bias.astype(f32)
    active = jax.nn.gelu(up_proj, approximate=True).astype(bf16)
    down_part = jnp.dot(active, down_weight, preferred_element_type=f32)
    down_local = lax.psum_scatter(
        down_part.astype(jnp.bfloat16), "tensor", scatter_dimension=1, tiled=True
    ).astype(jnp.float32)
    outputs = (resid_local + down_local + down_bias.astype(f32)).astype(bf16)
    grad_full = lax.all_gather(grad_out, "tensor", axis=1, tiled=True)
    grad_local_f = grad_out.astype(f32)
    grad_down_weight = jnp.einsum("sf,sd->fd", active, grad_full, preferred_element_type=f32)
    grad_down_bias = jnp.sum(grad_local_f, axis=0)
    grad_active = jnp.einsum("sd,fd->sf", grad_full, down_weight, preferred_element_type=f32)
    gelu_pull = jax.vjp(partial(jax.nn.gelu, approximate=True), up_proj)[1]
    grad_up_proj = gelu_pull(grad_active)[0].astype(bf16)
    grad_up_bias = jnp.sum(grad_up_proj, axis=0, dtype=f32)
    grad_up_weight = jnp.einsum("sd,sf->df", normed_two, grad_up_proj, preferred_element_type=f32)
    grad_normed_two = jnp.einsum("sf,df->sd", grad_up_proj, up_weight, preferred_element_type=f32)
    grad_two_local = lax.psum_scatter(
        grad_normed_two.astype(jnp.bfloat16), "tensor", scatter_dimension=1, tiled=True
    ).astype(jnp.float32)
    unit_two_local = lax.dynamic_slice_in_dim(unit_two, col_start, width_local, 1)
    grad_ffn_norm_gain = jnp.sum(grad_two_local * unit_two_local, axis=0)
    grad_ffn_norm_bias = jnp.sum(grad_two_local, axis=0)
    scaled_two = grad_two_local * ffn_norm_gain.astype(f32)
    sum_two, dot_two = lax.psum(
        (jnp.sum(scaled_two, axis=1), jnp.sum(scaled_two * unit_two_local, axis=1)), "tensor"
    )
    grad_resid_local = grad_local_f + inv_two * (
        scaled_two - sum_two[:, None] / D - unit_two_local * dot_two[:, None] / D
    )
    grad_out_bias = jnp.sum(grad_resid_local, axis=0)
    grad_branch = lax.all_gather(grad_resid_local.astype(bf16), "tensor", axis=1, tiled=True)
    grad_out_weight = jnp.einsum("sc,sd->cd", seq_context, grad_branch, preferred_element_type=f32)
    grad_context = jnp.einsum(
        "sd,cd->sc", grad_branch, out_weight, preferred_element_type=f32
    ).astype(bf16)
    grad_context_heads = grad_context.reshape(seq_count, LEN, heads_local, HD)
    seq_id = 0
    allowed_blocks, key_valid = masks_kept[seq_id]
    seq_q, seq_k, seq_v = attend_backward(
        query_heads[seq_id],
        key_heads[seq_id],
        val_heads[seq_id],
        grad_context_heads[seq_id],
        totals_kept[seq_id],
        allowed_blocks,
        key_valid,
    )
    grad_queries = seq_q.astype(bf16)
    grad_keys = seq_k.astype(bf16)
    grad_vals = seq_v.astype(bf16)
    grad_query_weight = jnp.einsum(
        "sd,sc->dc", normed_one, grad_queries, preferred_element_type=f32
    )
    grad_key_weight = jnp.einsum("sd,sc->dc", normed_one, grad_keys, preferred_element_type=f32)
    grad_value_weight = jnp.einsum("sd,sc->dc", normed_one, grad_vals, preferred_element_type=f32)
    grad_query_bias = jnp.sum(grad_queries, axis=0, dtype=f32)
    grad_value_bias = jnp.sum(grad_vals, axis=0, dtype=f32)
    grad_normed_one = (
        jnp.einsum("sc,dc->sd", grad_queries, query_weight, preferred_element_type=f32)
        + jnp.einsum("sc,dc->sd", grad_keys, key_weight, preferred_element_type=f32)
        + jnp.einsum("sc,dc->sd", grad_vals, value_weight, preferred_element_type=f32)
    )
    grad_one_local = lax.psum_scatter(
        grad_normed_one.astype(jnp.bfloat16), "tensor", scatter_dimension=1, tiled=True
    ).astype(jnp.float32)
    unit_one_local = lax.dynamic_slice_in_dim(unit_one, col_start, width_local, 1)
    grad_attn_norm_gain = jnp.sum(grad_one_local * unit_one_local, axis=0)
    grad_attn_norm_bias = jnp.sum(grad_one_local, axis=0)
    scaled_one = grad_one_local * attn_norm_gain.astype(f32)
    sum_one, dot_one = lax.psum(
        (jnp.sum(scaled_one, axis=1), jnp.sum(scaled_one * unit_one_local, axis=1)), "tensor"
    )
    grad_inputs = (
        grad_resid_local
        + inv_one * (scaled_one - sum_one[:, None] / D - unit_one_local * dot_one[:, None] / D)
    ).astype(bf16)
    (
        grad_attn_norm_gain,
        grad_attn_norm_bias,
        grad_query_weight,
        grad_query_bias,
        grad_key_weight,
        grad_value_weight,
        grad_value_bias,
        grad_out_weight,
        grad_out_bias,
        grad_ffn_norm_gain,
        grad_ffn_norm_bias,
        grad_up_weight,
        grad_up_bias,
        grad_down_weight,
        grad_down_bias,
    ) = lax.psum(
        (
            grad_attn_norm_gain,
            grad_attn_norm_bias,
            grad_query_weight,
            grad_query_bias,
            grad_key_weight,
            grad_value_weight,
            grad_value_bias,
            grad_out_weight,
            grad_out_bias,
            grad_ffn_norm_gain,
            grad_ffn_norm_bias,
            grad_up_weight,
            grad_up_bias,
            grad_down_weight,
            grad_down_bias,
        ),
        "dp",
    )
    return (
        outputs,
        grad_inputs,
        grad_attn_norm_gain,
        grad_attn_norm_bias,
        grad_query_weight,
        grad_query_bias,
        grad_key_weight,
        grad_value_weight,
        grad_value_bias,
        grad_out_weight,
        grad_out_bias,
        grad_ffn_norm_gain,
        grad_ffn_norm_bias,
        grad_up_weight,
        grad_up_bias,
        grad_down_weight,
        grad_down_bias,
    )


def solution(mesh):
    return jax.shard_map(
        shards,
        mesh=mesh,
        in_specs=(
            P("dp", "tensor"),
            P("dp"),
            P("dp", "tensor", None, None),
            P("tensor"),
            P("tensor"),
            P(None, "tensor"),
            P("tensor"),
            P(None, "tensor"),
            P(None, "tensor"),
            P("tensor"),
            P("tensor", None),
            P("tensor"),
            P("tensor"),
            P("tensor"),
            P(None, "tensor"),
            P("tensor"),
            P("tensor", None),
            P("tensor"),
            P("dp", "tensor"),
        ),
        out_specs=(
            P("dp", "tensor"),
            P("dp", "tensor"),
            P("tensor"),
            P("tensor"),
            P(None, "tensor"),
            P("tensor"),
            P(None, "tensor"),
            P(None, "tensor"),
            P("tensor"),
            P("tensor", None),
            P("tensor"),
            P("tensor"),
            P("tensor"),
            P(None, "tensor"),
            P("tensor"),
            P("tensor", None),
            P("tensor"),
        ),
        check_vma=False,
    )
```

profile of v0, /device:TPU:0, one launch (start us, length us, event | category | flops | bytes accessed | tf_op | source)
XLA Modules:
  0.0 715.1 jit_solution(1099334887405132671)
XLA Ops:
  14.3 14.9 %all_gather.13 = bf16[6,1024]{1,0:T(8,128)(2,1)S(1)} all-gather(bf16[6,256]{1,0:T(8,128)(2,1)S(1)} %stack.27), channel_id=1, replica_groups=mesh['dp'=8,'tensor'=4] {'tensor'}, dimensions={1}, use_global_device_ids=true | all-gather | bytes 15360 | tf_op jit(solution)/shard_map/all_gather | solution.py:139
  29.2 29.5 %all-gather.4.cloned.1.call-done = bf16[1024,1024]{1,0:T(8,128)(2,1)} async-done(((bf16[1024,256]{1,0:T(8,128)(2,1)}), bf16[1024,1024]{1,0:T(8,128)(2,1)}) %all-gather.4.cloned.1.call-update) | async-done | bytes 2097168 | tf_op jit(solution)/shard_map/all_gather | solution.py:138
  69.2 33.2 %while.28 = (s32[]{:T(128)}, bf16[2,512,4,64]{1,3,2,0:T(8,128)(2,1)}, f32[2,4,512]{2,1,0:T(4,128)S(1)}, s32[2]{0:T(128)S(1)}, pred[4,16,16]{1,2,0:T(8,128)(4,1)S...) while((s32[]{:T(128)}, ...), condition=%wide.region_6.7_spmd.clone, body=%wide.region_3.6_spmd.clone.sunk | while | flops 568458240 | bytes 45815652 | solution.py:63
  72.7 4.0 copy.53
  89.2 4.0 copy.53
  104.8 3.8 fusion.76
  109.6 152.4 %all-reduce.7.cloned.1.call-done = f32[1024,1024]{1,0:T(8,128)} async-done(((f32[1024,1024]{1,0:T(8,128)}), f32[1024,1024]{1,0:T(8,128)}) %all-reduce.7.cloned.1.call-update) | async-done | bytes 4194320 | tf_op jit(solution)/shard_map/psum | solution.py:171
  269.4 4.4 fusion.66
  273.8 35.1 %all-gather.6.cloned.1.call-done = bf16[1024,1024]{1,0:T(8,128)(2,1)} async-done(((bf16[1024,256]{1,0:T(8,128)(2,1)}), bf16[1024,1024]{1,0:T(8,128)(2,1)}) %all-gather.6.cloned.1.call-update) | async-done | bytes 2097168 | tf_op jit(solution)/shard_map/all_gather | solution.py:183
  308.9 8.1 %convert_reduce_fusion.1 = (f32[1024]{0:T(1024)}, bf16[1024,1024]{1,0:T(8,128)(2,1)S(1)}) fusion(f32[1024,1024]{1,0:T(8,128)} %fusion.66, f32[1024]{0:T(1024)S(1)} %convert_element_type.133, bf16[1024,1024]{1,0:T(8,128)(2,1)} %all-gather.6.cloned.1.call-done, bf16[1024,1024]{1,0:T(8,128)(2,1)S(1)} %copy-done), kind=kOutput, calls=%fused_computation.60 | convolution fusion | flops 2171599872 | bytes 10493952 | tf_op jit(solution)/shard_map/sd,fd->sf/dot_general | solution.py:187
  318.3 3.7 convolution_convert_fusion
  322.1 42.2 %reduce-scatter.6.cloned.1.call-done = bf16[1024,256]{1,0:T(8,128)(2,1)} async-done(((bf16[1024,1024]{1,0:T(8,128)(2,1)}), bf16[1024,256]{1,0:T(8,128)(2,1)}) %reduce-scatter.6.cloned.1.call-update) | async-done | bytes 524304 | tf_op jit(solution)/shard_map/reduce_scatter | solution.py:193
  366.7 10.0 %all-reduce.3 = (f32[1024]{0:T(1024)S(1)}, f32[1024]{0:T(1024)S(1)}) all-reduce(f32[1024]{0:T(1024)S(1)} %get-tuple-element.219, f32[1024]{0:T(1024)S(1)} %get-tuple-element.223), channel_id=1, replica_groups=mesh['dp'=8,'tensor'=4] {'tensor'}, use_global_device_ids=true, to_apply=%region_15.16 | all-reduce | flops 2048 | bytes 16384 | tf_op jit(solution)/shard_map/psum | solution.py:200
  381.3 6.3 convolution_convert_fusion.1
  387.9 38.0 %all-gather.8.cloned.1.call-done = bf16[1024,1024]{1,0:T(8,128)(2,1)} async-done(((bf16[1024,256]{1,0:T(8,128)(2,1)}), bf16[1024,1024]{1,0:T(8,128)(2,1)}) %all-gather.8.cloned.1.call-update) | async-done | bytes 2097168 | tf_op jit(solution)/shard_map/all_gather | solution.py:207
  429.1 37.6 %while.29 = (s32[]{:T(128)}, f32[1024,4,64]{0,2,1:T(8,128)S(1)}, f32[1024,4,64]{0,2,1:T(8,128)S(1)}, bf16[2,512,4,64]{1,3,2,0:T(8,128)(2,1)}, s32[2]{0:T(128)S(1...) while((s32[]{:T(128)}, f32[1024,4,64]{0,2,1:T(8,128)S(1)}, ...), condition=%wide.region_18.19_spmd.clone, body=%wide.region_16.18_spmd.clone.sunk | while | flops 1364589568 | bytes 87207896 | solution.py:101
  434.6 4.0 copy.54
  453.4 4.0 copy.54
  472.9 7.4 %fusion.65 = f32[1024,1024]{1,0:T(8,128)} fusion(bf16[1024,1024]{1,0:T(8,128)(2,1)} %copy-done.53, f32[1024,1024]{1,0:T(8,128)} %copy-done.11, f32[1024]{0:T(1024)S(1)} %bitcast.158, f32[1024]{0:T(1024)S(1)} %bitcast.156), kind=kOutput, calls=%fused_computation.102 | convolution fusion | flops 2150629376 | bytes 10493952 | tf_op jit(solution)/shard_map/sd,sf->df/dot_general | solution.py:191
  480.3 5.1 fusion.70
  495.9 20.0 %reduce-scatter.8.cloned.1.call-done = bf16[1024,256]{1,0:T(8,128)(2,1)} async-done(((bf16[1024,1024]{1,0:T(8,128)(2,1)}), bf16[1024,256]{1,0:T(8,128)(2,1)}) %reduce-scatter.8.cloned.1.call-update) | async-done | bytes 524304 | tf_op jit(solution)/shard_map/reduce_scatter | solution.py:239
  517.7 24.7 %all-reduce = (f32[256]{0:T(256)}, f32[256]{0:T(256)}, f32[256]{0:T(256)}, f32[256]{0:T(256)}, f32[256]{0:T(256)}, /*index=5*/f32[256]{0:T(256)}, f32[256]{0:T(256)}, f32[1024]{0:T(1024)}, f32[256]{0:T(256)}) all-reduce(f32[256]{0:T(256)S(1)} %get-tuple-element.220, ...), channel_id=1, replica_groups=mesh['dp'=8,'tensor'=4] {'dp'}, use_global_device_ids=true, to_apply=%region_25.26 | all-reduce | flops 3072 | bytes 24576 | tf_op jit(solution)/shard_map/psum | solution.py:269
  542.5 10.3 %all-reduce.2 = (f32[1024]{0:T(1024)S(1)}, f32[1024]{0:T(1024)S(1)}) all-reduce(f32[1024]{0:T(1024)S(1)} %get-tuple-element.221, f32[1024]{0:T(1024)S(1)} %get-tuple-element.222), channel_id=1, replica_groups=mesh['dp'=8,'tensor'=4] {'tensor'}, use_global_device_ids=true, to_apply=%region_23.24 | all-reduce | flops 2048 | bytes 16384 | tf_op jit(solution)/shard_map/psum | solution.py:246
  555.5 139.8 %all-reduce.9.cloned.1.call-done = (f32[1024,256]{1,0:T(8,128)}, f32[1024,256]{1,0:T(8,128)}, f32[1024,256]{1,0:T(8,128)}, f32[256,1024]{1,0:T(8,128)}, f32[1024,1024]{1,0:T(8,128)}, /*index=5*/f32[1024,1024]{1,0:T(8,128)}) async-done(((f32[1024,256]{1,0:T(8,128)}, f32[1024,256]{1,0:T(8,128)}, f32[1024,256]{1,0:T(8,128)}, f32[256,1024]{1,0:T(8,128)}, f32[1024,1024]{1,0:T(8,128)}, ...) | async-done | bytes 12582928 | tf_op jit(solution)/shard_map/psum | solution.py:269
  (257 shorter events, 118.6 us)
Async XLA Ops:
  7.2 301.7 %copy-start = (bf16[1024,1024]{1,0:T(8,128)(2,1)S(1)}, bf16[1024,1024]{1,0:T(8,128)(2,1)}, u32[]{:S(2)}) copy-start(bf16[1024,1024]{1,0:T(8,128)(2,1)} %param.39) | copy-start | bytes 6291460
  7.2 51.5 %all-gather.4.cloned.1.call-start = ((), (), s32[]{:S(2)}) async-start(), calls=%async_computation.3 | async-start | bytes 2621440 | tf_op jit(solution)/shard_map/all_gather | solution.py:138
  7.9 254.1 %all-reduce.7.cloned.1.call-start = ((), (), s32[]{:S(2)}) async-start(), calls=%async_computation.4 | async-start | bytes 8388608 | tf_op jit(solution)/shard_map/psum | solution.py:171
  29.2 238.2 %copy-start.40 = (f32[1,1024]{1,0:T(1,128)}, f32[1,1024]{1,0:T(1,128)S(1)}, u32[]{:S(2)}) copy-start(f32[1,1024]{1,0:T(1,128)S(1)} %get-tuple-element.302) | copy-start | bytes 12292
  29.2 238.2 %copy-start.42 = (f32[1,1024]{1,0:T(1,128)}, f32[1,1024]{1,0:T(1,128)S(1)}, u32[]{:S(2)}) copy-start(f32[1,1024]{1,0:T(1,128)S(1)} %get-tuple-element.303) | copy-start | bytes 12292
  108.6 200.3 %all-gather.6.cloned.1.call-start = ((), (), s32[]{:S(2)}) async-start(), calls=%async_computation.6 | async-start | bytes 2621440 | tf_op jit(solution)/shard_map/all_gather | solution.py:183
  109.4 254.9 %reduce-scatter.6.cloned.1.call-start = ((), (), s32[]{:S(2)}) async-start(), calls=%async_computation.7 | async-start | bytes 2621440 | tf_op jit(solution)/shard_map/reduce_scatter | solution.py:193
  308.9 9.4 %copy-start.47 = (bf16[1024,1024]{1,0:T(8,128)(2,1)S(1)}, bf16[1024,1024]{1,0:T(8,128)(2,1)}, u32[]{:S(2)}) copy-start(bf16[1024,1024]{1,0:T(8,128)(2,1)} %param.37) | copy-start | bytes 6291460
  322.0 103.9 %all-gather.8.cloned.1.call-start = ((), (), s32[]{:S(2)}) async-start(), calls=%async_computation.8 | async-start | bytes 2621440 | tf_op jit(solution)/shard_map/all_gather | solution.py:207
  381.3 111.8 %reduce-scatter.4.cloned.1.call-start = ((), (), s32[]{:S(2)}) async-start(), calls=%async_computation.5 | async-start | bytes 2621440 | tf_op jit(solution)/shard_map/reduce_scatter | solution.py:179
  387.7 41.5 %copy-start.2 = (f32[1024,4,64]{0,2,1:T(8,128)S(1)}, f32[1024,4,64]{0,2,1:T(8,128)}, u32[]{:S(2)}) copy-start(f32[1024,4,64]{0,2,1:T(8,128)} %custom-call) | copy-start | bytes 3145732
  387.7 41.5 %copy-start.6 = (f32[1024,4,64]{0,2,1:T(8,128)S(1)}, f32[1024,4,64]{0,2,1:T(8,128)}, u32[]{:S(2)}) copy-start(f32[1024,4,64]{0,2,1:T(8,128)} %custom-call.1) | copy-start | bytes 3145732
  387.7 128.1 %reduce-scatter.8.cloned.1.call-start = ((), (), s32[]{:S(2)}) async-start(), calls=%async_computation.9 | async-start | bytes 2621440 | tf_op jit(solution)/shard_map/reduce_scatter | solution.py:239
  472.6 222.8 %all-reduce.9.cloned.1.call-start = ((), (), s32[]{:S(2)}) async-start(), calls=%async_computation.10 | async-start | bytes 25165824 | tf_op jit(solution)/shard_map/psum | solution.py:269
  472.9 7.4 %copy-start.48 = (bf16[1024,1024]{1,0:T(8,128)(2,1)S(1)}, bf16[1024,1024]{1,0:T(8,128)(2,1)}, u32[]{:S(2)}) copy-start(bf16[1024,1024]{1,0:T(8,128)(2,1)} %all-gather.6.cloned.1.call-done) | copy-start | bytes 6291460
  472.9 7.4 %copy-start.52 = (f32[1024,1024]{1,0:T(8,128)S(1)}, f32[1024,1024]{1,0:T(8,128)}, u32[]{:S(2)}) copy-start(f32[1024,1024]{1,0:T(8,128)} %fusion.66) | copy-start | bytes 12582916
  493.0 24.7 %copy-start.36 = (f32[256]{0:T(256)S(1)}, f32[256]{0:T(256)}, u32[]{:S(2)}) copy-start(f32[256]{0:T(256)} %get-tuple-element.218) | copy-start | bytes 3076
  493.0 24.7 %copy-start.37 = (f32[256]{0:T(256)S(1)}, f32[256]{0:T(256)}, u32[]{:S(2)}) copy-start(f32[256]{0:T(256)} %get-tuple-element.224) | copy-start | bytes 3076
  493.0 24.7 %copy-start.38 = (f32[256]{0:T(256)S(1)}, f32[256]{0:T(256)}, u32[]{:S(2)}) copy-start(f32[256]{0:T(256)} %get-tuple-element.289) | copy-start | bytes 3076
  493.0 24.7 %copy-start.39 = (f32[256]{0:T(256)S(1)}, f32[256]{0:T(256)}, u32[]{:S(2)}) copy-start(f32[256]{0:T(256)} %get-tuple-element.301) | copy-start | bytes 3076
  493.0 24.7 %copy-start.44 = (f32[1024]{0:T(1024)S(1)}, f32[1024]{0:T(1024)}, u32[]{:S(2)}) copy-start(f32[1024]{0:T(1024)} %get-tuple-element.287) | copy-start | bytes 12292
  493.0 59.8 %copy-start.13 = (f32[1024,256]{1,0:T(8,128)S(1)}, f32[1024,256]{1,0:T(8,128)}, u32[]{:S(2)}) copy-start(f32[1024,256]{1,0:T(8,128)} %copy-done.12) | copy-start | bytes 3145732
  493.0 59.8 %copy-start.35 = (f32[1024]{0:T(1024)S(1)}, f32[1024]{0:T(1024)}, u32[]{:S(2)}) copy-start(f32[1024]{0:T(1024)} %copy-done.34) | copy-start | bytes 12292
  695.4 6.7 copy-start.19
  (45 other events, 119.5 us)
Sparse Core Ops, SparseCore 0:
  9.6 49.0 all-gather.3
  108.8 153.1 all-reduce.6
  263.6 45.2 all-gather.5
  322.2 42.0 reduce-scatter.5
  381.4 44.4 all-gather.7
  428.1 42.1 reduce-scatter.3
  472.7 43.1 reduce-scatter.7
  521.6 173.7 all-reduce.8
where the time goes:
time: 724 us; the launch traced here: 715 us
  waiting for transfers between devices  458 us (63%)
  matrix products  83.1 us (11%)
  blocking collectives  59.9 us (8%)
  local copies, waits for them, and re-layouts  51.5 us (7%)
  other arithmetic  36.4 us (5%)
  between operations  15.2 us (2%)
  loops' own time  9.58 us (1%)
    psum x1, waiting for transfers between devices, shards(): attn_full = lax.psum(attn_part, 'tensor')  152 us
    psum x1, waiting for transfers between devices, shards(): lax.psum((grad_attn_norm_gain, grad_attn_norm_bias, grad_query_weight, gr...  140 us
    reduce_scatter x1, waiting for transfers between devices, shards(): lax.psum_scatter(grad_normed_two.astype(jnp.bfloat16), 'tensor', scatter_...  42.2 us
    all_gather x1, waiting for transfers between devices, shards(): lax.all_gather(grad_resid_local.astype(bf16), 'tensor', axis=1, tiled=True)  38 us
    all_gather x1, waiting for transfers between devices, shards(): grad_full = lax.all_gather(grad_out, 'tensor', axis=1, tiled=True)  35.1 us
    all_gather x1, waiting for transfers between devices, shards(): lax.all_gather(inputs, 'tensor', axis=1, tiled=True)  29.5 us
    psum x1, blocking collectives, shards(): lax.psum((grad_attn_norm_gain, grad_attn_norm_bias, grad_query_weight, gr...  24.7 us
    reduce_scatter x1, waiting for transfers between devices, shards(): lax.psum_scatter(grad_normed_one.astype(jnp.bfloat16), 'tensor', scatter_...  20 us
  transfers between devices with their start and end apart: 8, of which 7 were waited for; matrix products, arithmetic and copies ran while one was open for 12% of the time, Pallas kernels for 0%

commit v1 on v0

v1 whole, which is shorter than its diff:
```python
from functools import partial

import jax
import jax.numpy as jnp
from jax import lax
from jax.experimental import pallas as pl
from jax.experimental.pallas import tpu as pltpu
from jax.sharding import PartitionSpec as P

D = 1024
HD = 64
BLOCK = 64
LEN = 1024
NB = 16
EPS = 1e-05
VMEM_LIMIT = 60 * 1024 * 1024
f32 = jnp.float32
bf16 = jnp.bfloat16
NT = (((1,), (1,)), ((), ()))
NN = (((1,), (0,)), ((), ()))
TN = (((0,), (0,)), ((), ()))


def mm(left, right, dims=NN):
    return lax.dot_general(left, right, dims, preferred_element_type=f32)


def call(kernel, name, grid, in_specs, out_specs, out_shape, scratch=(), flops=0, nbytes=0,
         aliases=None):
    return pl.pallas_call(
        kernel,
        out_shape=out_shape,
        grid_spec=pltpu.PrefetchScalarGridSpec(
            num_scalar_prefetch=1,
            grid=grid,
            in_specs=in_specs,
            out_specs=out_specs,
            scratch_shapes=list(scratch),
        ),
        compiler_params=pltpu.CompilerParams(
            dimension_semantics=("arbitrary",) * len(grid), vmem_limit_bytes=VMEM_LIMIT
        ),
        cost_estimate=pl.CostEstimate(flops=0, bytes_accessed=0, transcendentals=0),
        input_output_aliases=aliases or {},
        name=name,
    )


def sds(shape, dtype):
    return jax.ShapeDtypeStruct(shape, dtype)


def const(shape):
    return pl.BlockSpec(shape, lambda i, z: (0,) * len(shape))


def rows_of(shape):
    return pl.BlockSpec(shape, lambda i, z: (i,) + (0,) * (len(shape) - 1))


def lane_ds(start, size):
    return pl.ds(pl.multiple_of(start, 128), size)


def across(value, mask, size):
    return lax.ppermute(value, "tensor", [(i, i ^ mask) for i in range(size)])


def swap(value, mask, size):
    return lax.ppermute(value, "dp", [(i, i ^ mask) for i in range(size)])


def gather4(value, size):
    far = across(value, 2, size)
    near = across(value, 1, size)
    return [value, near, far, across(far, 1, size)]


def scatter4(slots, size):
    got3 = across(slots[3], 1, size)
    got1 = across(slots[1], 1, size)
    far = (slots[2].astype(f32) + got3.astype(f32)).astype(slots[2].dtype)
    return slots[0], got1, across(far, 2, size)


def sum4(value, size):
    value = value + across(value, 1, size)
    return value + across(value, 2, size)


def stages(size):
    bits = list(range(size.bit_length() - 1))
    return [bits[:1]] + [bits[j:j + 2] for j in range(1, len(bits), 2)]


def digit_of(index, group):
    digit = 0
    for j, bit in enumerate(group):
        digit = digit | (((index >> bit) & 1) << j)
    return digit


def mask_of(k, group):
    return sum(((k >> j) & 1) << bit for j, bit in enumerate(group))


def dp_position(size):
    index = lax.axis_index("dp")
    place = 0
    for group in stages(size):
        place = (place << len(group)) | digit_of(index, group)
    return place.astype(jnp.int32)


def dp_scatter(value, size, axis=0, groups=None):
    index = lax.axis_index("dp")
    for group in stages(size) if groups is None else groups:
        n = 1 << len(group)
        mine = digit_of(index, group)
        rows = value.shape[axis] // n
        take = lambda at: lax.dynamic_slice_in_dim(value, at * rows, rows, axis)
        got = [swap(take(mine ^ k), mask_of(k, group), size) for k in range(1, n)]
        total = take(mine).astype(f32)
        for g in got:
            total = total + g.astype(f32)
        value = total.astype(value.dtype)
    return value


def dp_gather(value, size, groups=None):
    value = value[None]
    for group in (stages(size) if groups is None else groups)[::-1]:
        n = 1 << len(group)
        value = jnp.stack([value] + [swap(value, mask_of(k, group), size) for k in range(1, n)])
        value = value.reshape((-1,) + value.shape[2:])
    return value


def dp_sum_small(value, size):
    for bit in range(size.bit_length() - 1):
        value = value + swap(value, 1 << bit, size)
    return value


def k_place(p_ref, value, *outs):
    w = outs[0].shape[-1]
    for j, out in enumerate(outs):
        out[...] = value[0][..., j * w:(j + 1) * w].astype(out.dtype)


def placed(value, size, dtype, outs=1, axis=0):
    n = value.shape[0]
    block = list(value.shape[1:])
    if block[axis] % 16:
        ordered = value[jnp.bitwise_xor(jnp.arange(n, dtype=jnp.int32), dp_position(size))]
        ordered = jnp.moveaxis(ordered, 0, axis)
        shape = block[:axis] + [n * block[axis]] + block[axis + 1:]
        return jnp.split(ordered.reshape(shape).astype(dtype), outs, axis=-1)
    block[-1] //= outs
    whole = list(block)
    whole[axis] *= n
    index = lambda i, p: tuple(
        jnp.bitwise_xor(i, p[0]) if d == axis else 0 for d in range(len(block)))
    return call(
        k_place, "place", (n,),
        [pl.BlockSpec((1,) + tuple(value.shape[1:]), lambda i, p: (i,) + (0,) * len(block))],
        [pl.BlockSpec(tuple(block), index)] * outs, [sds(tuple(whole), dtype)] * outs,
        nbytes=6 * value.size,
    )(dp_position(size).reshape(1), value)


def k_place_two(p_ref, one, two, up, down):
    first = p_ref[1] == 0
    up[...] = jnp.where(first, one[0], two[0]).astype(f32)
    down[...] = jnp.where(first, two[0], one[0]).astype(f32)


def dp_sum_two(up, down, size):
    groups = stages(size)
    side = digit_of(lax.axis_index("dp"), groups[0])
    sent = jnp.where(side == 0, down, up)
    kept = jnp.where(side == 0, up, down)
    part = (kept.astype(f32) + swap(sent, 1, size).astype(f32)).astype(bf16)
    part = dp_scatter(part, size, groups=groups[1:])
    one = dp_gather(part, size, groups=groups[1:])
    return one


def dp_sum_two_end(one, size):
    groups = stages(size)
    side = digit_of(lax.axis_index("dp"), groups[0])
    two = swap(one, 1, size)
    n, rows, cols = one.shape
    block = pl.BlockSpec((1, rows, cols), lambda i, p: (i, 0, 0))
    place = pl.BlockSpec((rows, cols), lambda i, p: (jnp.bitwise_xor(i, p[0] % n), 0))
    return call(
        k_place_two, "place_two", (n,), [block, block], [place, place],
        [sds((n * rows, cols), f32)] * 2, nbytes=12 * n * rows * cols,
    )(jnp.stack([dp_position(size), side.astype(jnp.int32)]), one, two)


def norm_stats(x):
    m = jnp.mean(x, axis=-1, keepdims=True)
    c = x - m
    r = lax.rsqrt(jnp.mean(c * c, axis=-1, keepdims=True) + EPS)
    return m, c, r


def k_qkv(z_ref, x0, x1, x2, x3, s0, s1, s2, s3, wq, wk, wv,
          x_out, n_out, q_out, k_out, v_out, nl_out, r_out, g_out):
    z = z_ref[0]
    w = x0.shape[1]
    for r, (xb, s) in enumerate(((x0, s0), (x1, s1), (x2, s2), (x3, s3))):
        at = lane_ds(jnp.bitwise_xor(z, r) * w, w)
        x_out[:, at] = xb[...]
        g_out[:, at] = s[...].astype(f32)
    m, c, r = norm_stats(x_out[...].astype(f32))
    n = (c * r * g_out[0:1, :] + g_out[1:2, :]).astype(bf16)
    n_out[...] = n
    nl_out[...] = (x0[...].astype(f32) - m) * r
    r_out[...] = jnp.broadcast_to(r, r_out.shape)
    small = s0[...].astype(f32)
    q_out[...] = ((mm(n, wq[...]) + small[5:6, :]).astype(bf16) * 0.125).astype(bf16)
    k_out[...] = mm(n, wk[...]).astype(bf16)
    v_out[...] = (mm(n, wv[...]) + small[6:7, :]).astype(bf16)


def low_lanes(shape):
    return lax.broadcasted_iota(jnp.int32, shape, len(shape) - 1) < HD


def k_attend(z_ref, q, k, v, bias, ctx_out, p_out):
    rows = q.shape[0]
    nblk = rows // BLOCK
    low = low_lanes((rows, 2 * HD))
    heads = q.shape[1] // HD
    for pair in range(heads // 2):
        lanes = slice(pair * 2 * HD, (pair + 1) * 2 * HD)
        qp = q[:, lanes]
        kp = k[:, lanes]
        vp = v[:, lanes]
        parts = []
        for side in range(2):
            h = pair * 2 + side
            qm = jnp.where(low if side == 0 else ~low, qp, jnp.zeros_like(qp))
            s = mm(qm, kp, NT)
            pieces = []
            for b in range(nblk):
                sb = s[b * BLOCK:(b + 1) * BLOCK] + bias[b * heads + h:b * heads + h + 1, :]
                top = jnp.max(sb, axis=-1, keepdims=True)
                e = jnp.exp(sb - top)
                total = jnp.sum(e, axis=-1, keepdims=True)
                pieces.append((e * (1.0 / total)).astype(bf16))
            p = jnp.concatenate(pieces, 0)
            p_out[h] = p
            parts.append(mm(p, vp))
        ctx_out[:, lanes] = jnp.where(low, parts[0], parts[1]).astype(bf16)


def k_ffn(base, z_ref, c0, c1, c2, c3, g0, g1, g2, g3, x, gains, wo0, wo, wu, ub, wd, *rest):
    (go_out, res_out, n_out, act_out, gup_out, d0, d1, d2, d3,
     h0, h1, h2, h3, sums_out) = rest[-14:]
    i = pl.program_id(0)
    z = z_ref[0]
    w = c0.shape[1]
    attn = mm(c0[...], wo0[...])
    for r, c in enumerate((c1, c2, c3)):
        attn = attn + mm(c[...], wo[r])
    for r, g in enumerate((g0, g1, g2, g3)):
        go_out[:, lane_ds(jnp.bitwise_xor(z, r) * w, w)] = g[...]
    resid = x[...].astype(f32) + attn + gains[2:3, :]
    res_out[...] = resid
    m, c, r = norm_stats(resid)
    n = (c * r * gains[3:4, :] + gains[4:5, :]).astype(bf16)
    n_out[...] = n
    u = mm(n, wu[...]) + ub[...].astype(f32)
    uu = u * u
    t = jnp.tanh(0.7978845608028654 * u * (1.0 + 0.044715 * uu))
    half = 0.5 * (1.0 + t)
    act = (u * half).astype(bf16)
    slope = half + 0.5 * u * (1.0 - t * t) * (0.7978845608028654 * (1.0 + 0.134145 * uu))
    act_out[...] = act
    gup = (mm(go_out[...], wd[...], NT) * slope).astype(bf16)
    gup_out[...] = gup
    gnt = mm(gup, wu[...], NT).astype(bf16)
    seg = h0.shape[0]
    per = gnt.shape[0] // seg
    for s in range(per):
        for r, h in enumerate((h0, h1, h2, h3)):
            @pl.when(jnp.bitwise_xor(i * per + s, z) == r)
            def _():
                h[...] = gnt[s * seg:(s + 1) * seg]

    own = lane_ds(z * w, w)
    d0[...] = res_out[:, own] + mm(act, wd[:, own]) + gains[7:8, own]
    for r, d in ((1, d1), (2, d2), (3, d3)):
        d[...] = mm(act, wd[:, lane_ds(jnp.bitwise_xor(z, r) * w, w)]).astype(bf16)

    @pl.when(i == 0)
    def _():
        sums_out[...] = jnp.zeros_like(sums_out)

    sums_out[0:1, :] += jnp.sum(gup.astype(f32), axis=0, keepdims=True)
    sums_out[1:2, 0:w] += jnp.sum(g0[...].astype(f32), axis=0, keepdims=True)


def k_norm_two(z_ref, h0, h1, h2, resid, go, gains, wo0, wo, gr_out, gb_out, o0, o1, o2, o3, sums_out):
    gnt = h0[...].astype(f32) + h1[...].astype(f32) + h2[...].astype(f32)
    m, c, r = norm_stats(resid[...])
    n = c * r
    e = gnt * gains[3:4, :]
    me = jnp.mean(e, axis=-1, keepdims=True)
    mn = jnp.mean(e * n, axis=-1, keepdims=True)
    gres = go[...].astype(f32) + r * (e - me - n * mn)
    gr_out[...] = gres
    gb = gres.astype(bf16)
    gb_out[...] = gb
    sums_out[...] = jnp.zeros_like(sums_out)
    sums_out[0:1, :] = jnp.sum(gnt * n, axis=0, keepdims=True)
    sums_out[1:2, :] = jnp.sum(gnt, axis=0, keepdims=True)
    sums_out[2:3, :] = jnp.sum(gres, axis=0, keepdims=True)
    o0[...] = mm(gb, wo0[...], NT).astype(bf16)
    for k, o in enumerate((o1, o2, o3)):
        o[...] = mm(gb, wo[k], NT).astype(bf16)


def k_dw_out(z_ref, a0, a1, a2, a3, b0, b1, b2, b3, gb_a, gb_b, out):
    gb = jnp.concatenate([gb_a[...], gb_b[...]], axis=0)
    for r, (a, b) in enumerate(((a0, b0), (a1, b1), (a2, b2), (a3, b3))):
        out[r] = mm(jnp.concatenate([a[...], b[...]], axis=0), gb, TN).astype(bf16)


def k_dw_qkv(z_ref, n, gq, gk, gv, out):
    w = gq.shape[1]
    nv = n[...]
    for j, g in enumerate((gq, gk, gv)):
        out[:, j * w:(j + 1) * w] = mm(nv, g[...], TN).astype(bf16)


def k_attend_back(z_ref, q, k, v, p_a, p_b, ctx_a, ctx_b, e0, e1, e2, e3, f0, f1, f2, f3,
                  gq_out, gk_out, gv_out, sums_out, gc, gs, cx):
    z = z_ref[0]
    rows = e0.shape[0]
    total = q.shape[0]
    half = total // 2
    for h, es in enumerate(((e0, e1, e2, e3), (f0, f1, f2, f3))):
        for j, e in enumerate(es):
            at = h * half + jnp.bitwise_xor(z, j) * rows
            gc[pl.ds(pl.multiple_of(at, rows), rows), :] = e[...]
    cx[:half] = ctx_a[...]
    cx[half:] = ctx_b[...]
    low = low_lanes((total, 2 * HD))
    qp, kp, vp = q[...], k[...], v[...]
    gcv = gc[...]
    prod = gcv.astype(f32) * cx[...].astype(f32)
    gq, gk, gv = [], [], []
    for side in range(2):
        pick = low if side == 0 else ~low
        delta = jnp.sum(jnp.where(pick, prod, 0.0), axis=-1, keepdims=True)
        gm = jnp.where(pick, gcv, jnp.zeros_like(gcv))
        tile = 256
        for t in range(total // tile):
            at = slice(t * tile, (t + 1) * tile)
            gp = mm(gm[at], vp, NT)
            p = p_a if t * tile < half else p_b
            pt = p[side, t * tile % half:t * tile % half + tile, :].astype(f32)
            gs[at, :] = (pt * (gp - delta[at])).astype(bf16)
        gsv = gs[...]
        gq.append(mm(gsv, kp))
        gk.append(mm(qp, gsv, TN))
        gv.append(mm(gcv[:half], p_a[side], TN) + mm(gcv[half:], p_b[side], TN))
    gqv = (jnp.where(low, gq[0], gq[1]) * 0.125).astype(bf16)
    gq_out[...] = gqv
    top = lax.broadcasted_iota(jnp.int32, gk[0].shape, 0) < HD
    gk_out[...] = jnp.where(top, gk[0], gk[1]).T.astype(bf16)
    gvv = jnp.where(top, gv[0], gv[1]).T.astype(bf16)
    gv_out[...] = gvv
    sums_out[...] = jnp.zeros_like(sums_out)
    sums_out[0:1, :] = jnp.sum(gqv.astype(f32), axis=0, keepdims=True)
    sums_out[1:2, :] = jnp.sum(gvv.astype(f32), axis=0, keepdims=True)


def k_norm_one(z_ref, gq, gk, gv, wq, wk, wv, x, gains, gres_a, gres_b, o0, o1, o2, o3,
               stats_out, sums_out, scr):
    i = pl.program_id(0)
    z = z_ref[0]
    w = gq.shape[1]
    gn = mm(gq[...], wq[...], NT) + mm(gk[...], wk[...], NT) + mm(gv[...], wv[...], NT)
    m, c, r = norm_stats(x[...].astype(f32))
    n = c * r
    e = gn * gains[0:1, :]
    en = e * n
    se = jnp.sum(e, axis=-1, keepdims=True)
    de = jnp.sum(en, axis=-1, keepdims=True)
    lane = lax.broadcasted_iota(jnp.int32, (gn.shape[0], 128), 1)
    cols = jnp.where(lane == 0, se, jnp.where(lane == 1, de, 0.0))
    stats_out[...] = cols.T[0:8, :]
    scr[...] = r * e
    seg = gres_a.shape[0]
    rows = gn.shape[0]
    per_half = pl.num_programs(0) // 2
    for h, gres in enumerate((gres_a, gres_b)):
        @pl.when(i == h * per_half + (z * seg) // rows)
        def _():
            scr[pl.ds(pl.multiple_of((z * seg) % rows, seg), seg), :] += gres[...]

    for r, o in enumerate((o0, o1, o2, o3)):
        o[...] = scr[:, lane_ds(jnp.bitwise_xor(z, r) * w, w)].astype(bf16)

    @pl.when(i == 0)
    def _():
        sums_out[...] = jnp.zeros_like(sums_out)

    sums_out[0:1, :] += jnp.sum(gn * n, axis=0, keepdims=True)
    sums_out[1:2, :] += jnp.sum(gn, axis=0, keepdims=True)


def k_final(z_ref, t0, t1, t2, stats, nl, r, out):
    total = t0[...].astype(f32) + t1[...].astype(f32) + t2[...].astype(f32)
    cols = jnp.concatenate([stats[...]] * 16, 0).T * (1.0 / D)
    out[...] = (total - r[:, 0:1] * (cols[:, 0:1] + nl[...] * cols[:, 1:2])).astype(bf16)


def mask_bias(random_rows, length):
    heads = random_rows.shape[0]
    rows = jnp.arange(NB, dtype=jnp.int32)[:, None]
    cols = jnp.arange(NB, dtype=jnp.int32)[None, :]
    fixed = (
        (rows == 0) | (rows == NB - 1) | (cols == 0) | (cols == NB - 1)
        | (jnp.abs(rows - cols) <= 1)
    )
    chosen = jnp.any(random_rows[:, :, :, None] == cols[0][None, None, None, :], axis=2)
    allowed = jnp.transpose(fixed[None] | chosen, (1, 0, 2)).reshape(NB * heads, NB)
    valid = jnp.arange(LEN, dtype=jnp.int32) < length
    return jnp.where(jnp.repeat(allowed, BLOCK, axis=1) & valid[None, :], 0.0, -1e30).astype(f32)


def make_shards(dp, tp):
    def shards(inputs, lengths, random_blocks, attn_norm_gain, attn_norm_bias, query_weight,
               query_bias, key_weight, value_weight, value_bias, out_weight, out_bias,
               ffn_norm_gain, ffn_norm_bias, up_weight, up_bias, down_weight, down_bias, grad_out):
        tokens, w = inputs.shape
        ff = up_weight.shape[1]
        heads = w // HD
        half = tokens // 2
        quarter = tokens // tp
        tile = 256
        zi = lax.axis_index("tensor")
        z = zi.astype(jnp.int32).reshape(1)
        d_i = lax.axis_index("dp")

        seg = half // tp
        here_dp = dp_position(dp)
        part_rows = w // dp
        pack = D // dp
        zero = jnp.zeros((1, w), bf16)
        small = jnp.concatenate(
            [v.reshape(1, w) for v in (attn_norm_gain, attn_norm_bias, out_bias, ffn_norm_gain,
                                       ffn_norm_bias, query_bias, value_bias, down_bias)]
            + [zero] * 8, 0)
        wo_part = lax.dynamic_slice_in_dim(out_weight, here_dp * part_rows, part_rows, 0)
        first = jnp.concatenate([inputs, small, wo_part.reshape(pack, w)], 0)
        slots = gather4(first, tp)

        bias = mask_bias(random_blocks[0], lengths[0])

        tw, td = rows_of((tile, w)), rows_of((tile, D))
        small_at = pl.BlockSpec((16, w), lambda i, z: (tokens // 16, 0))
        x_full, n_one, q, k, v, n_loc, r_one, gains = call(
            k_qkv, "qkv", (tokens // tile,),
            [tw] * 4 + [small_at] * 4 + [const((D, w))] * 3,
            [td, td, tw, tw, tw, tw, rows_of((tile, 128)), const((16, D))],
            [sds((tokens, D), bf16), sds((tokens, D), bf16), sds((tokens, w), bf16),
             sds((tokens, w), bf16), sds((tokens, w), bf16), sds((tokens, w), f32),
             sds((tokens, 128), f32), sds((16, D), f32)],
            flops=2 * tokens * D * 3 * w, nbytes=12 << 20,
        )(z, *slots, *slots, query_weight, key_weight, value_weight)

        go_in, _ = lax.optimization_barrier((grad_out, slots[3]))
        gos = gather4(go_in, tp)

        nblk = tile // BLOCK
        att = []
        for h in range(2):
            steps = half // tile
            base = h * steps
            att.append(call(
                k_attend, "attend", (steps,),
                [pl.BlockSpec((tile, w), lambda i, z, base=base: (i + base, 0)),
                 const((tokens, w)), const((tokens, w)),
                 pl.BlockSpec((nblk * heads, LEN), lambda i, z, base=base: (i + base, 0))],
                [tw, pl.BlockSpec((heads, tile, LEN), lambda i, z: (0, i, 0))],
                [sds((half, w), bf16), sds((heads, half, LEN), bf16)],
                flops=2 * half * LEN * 128 * heads * 2, nbytes=8 << 20,
            )(z, q, k, v, bias))
        ctxs = [gather4(att[h][0], tp) for h in range(2)]

        wo_in = jnp.stack([s[tokens + 16:].reshape(part_rows, D) for s in slots[1:]])
        wo_in, _ = lax.optimization_barrier((wo_in, att[1][0]))
        (wo_rest,) = placed(dp_gather(wo_in, dp), dp, bf16, axis=1)

        ffn = []
        carried = []
        for h in range(2):
            steps = half // tile
            base = h * steps
            here = lambda i, z, base=base: (i + base, 0)
            hw, hd, hf = (pl.BlockSpec((tile, n), here) for n in (w, D, ff))
            n_in = 18
            out = call(
                partial(k_ffn, base), "ffn", (steps,),
                [tw] * 4 + [hw] * 4 + [hd, const((16, D)), const((w, D)), const((tp - 1, w, D)),
                                       const((D, ff)), const((1, ff)), const((ff, D))]
                + [pl.BlockSpec(memory_space=pl.ANY)] * len(carried),
                [hd, hd, hd, hf, hf, hw, hw, hw, hw] + [const((seg, D))] * 4 + [const((8, ff))],
                [sds((tokens, D), bf16), sds((tokens, D), f32), sds((tokens, D), bf16),
                 sds((tokens, ff), bf16), sds((tokens, ff), bf16), sds((tokens, w), f32)]
                + [sds((tokens, w), bf16)] * 3 + [sds((seg, D), bf16)] * 4 + [sds((8, ff), f32)],
                flops=2 * half * D * ff * 5, nbytes=24 << 20,
                aliases={16 + j: j for j in range(len(carried))},
            )(z, *ctxs[h], *gos, x_full, gains, out_weight, wo_rest, up_weight,
              up_bias.reshape(1, ff), down_weight, *carried)
            carried = out[:9]
            ffn.append(out)
        go_full, res_full, n_two, act, gup, d0, d1, d2, d3 = carried

        two = []
        for h in range(2):
            h0, h1, h2 = scatter4(ffn[h][9:13], tp)
            at_z = pl.BlockSpec((seg, D), lambda i, z, h=h: (h * tp + z[0], 0))
            two.append(call(
                k_norm_two, "norm_two", (1,),
                [const((seg, D))] * 3 + [at_z, at_z, const((16, D)), const((w, D)),
                                         const((tp - 1, w, D))],
                [const((seg, D)), const((seg, D))] + [const((seg, w))] * 4 + [const((8, D))],
                [sds((seg, D), f32), sds((seg, D), bf16)] + [sds((seg, w), bf16)] * 4
                + [sds((8, D), f32)],
                flops=2 * seg * D * D, nbytes=10 << 20,
            )(z, h0, h1, h2, res_full, go_full, gains, out_weight, wo_rest))
        g_ctx = [[two[h][2]] + [across(two[h][2 + r], r, tp) for r in range(1, tp)]
                 for h in range(2)]

        (d1, d2, d3), _ = lax.optimization_barrier(((d1, d2, d3), g_ctx[1]))
        outputs = sum(t.astype(f32) for t in scatter4([d0, d1, d2, d3], tp)).astype(bf16)

        pair = pl.BlockSpec((tokens, 2 * HD), lambda i, z: (0, i))
        pairh = pl.BlockSpec((half, 2 * HD), lambda i, z: (0, i))
        probs = pl.BlockSpec((2, half, LEN), lambda i, z: (i, 0, 0))
        gq, gk, gv, sums_qkv = call(
            k_attend_back, "attend_back", (heads // 2,),
            [pair, pair, pair, probs, probs, pairh, pairh]
            + [pl.BlockSpec((seg, 2 * HD), lambda i, z: (0, i))] * 8,
            [pair, pair, pair, pl.BlockSpec((8, 2 * HD), lambda i, z: (0, i))],
            [sds((tokens, w), bf16)] * 3 + [sds((8, w), f32)],
            scratch=[pltpu.VMEM((tokens, 2 * HD), bf16), pltpu.VMEM((tokens, LEN), bf16),
                     pltpu.VMEM((tokens, 2 * HD), bf16)],
            flops=2 * tokens * LEN * 128 * heads * 4, nbytes=12 << 20,
        )(z, q, k, v, att[0][1], att[1][1], att[0][0], att[1][0], *g_ctx[0], *g_ctx[1])

        *contrib, stats, sums_one = call(
            k_norm_one, "norm_one", (tokens // tile,),
            [tw] * 3 + [const((D, w))] * 3 + [td, const((16, D)), const((seg, D)), const((seg, D))],
            [tw] * 4 + [pl.BlockSpec((8, tile), lambda i, z: (0, i)), const((8, D))],
            [sds((tokens, w), bf16)] * 4 + [sds((8, tokens), f32), sds((8, D), f32)],
            scratch=[pltpu.VMEM((tile, D), f32)],
            flops=2 * tokens * D * 3 * w, nbytes=12 << 20,
        )(z, gq, gk, gv, query_weight, key_weight, value_weight, x_full, gains, two[0][0], two[1][0])

        totals = scatter4(contrib, tp)
        sums_two = two[0][6] + two[1][6]
        mix = jnp.concatenate([stats[0:2], sums_one[0:2], sums_two[0:3], jnp.zeros((1, D), f32)], 0)
        mix = sum4(mix, tp)
        grad_inputs = call(
            k_final, "final", (tokens // tile,),
            [tw] * 3 + [pl.BlockSpec((8, tile), lambda i, z: (0, i)), tw, rows_of((tile, 128))],
            tw, sds((tokens, w), bf16), flops=tokens * w * 8, nbytes=5 << 20,
        )(z, *totals, mix, n_loc, r_one)

        dw_up = mm(n_two, gup, TN).astype(bf16)
        dw_down = mm(act, go_full, TN).astype(bf16)
        g_up, g_down = dp_sum_two_end(dp_sum_two(dw_up, dw_down, dp), dp)

        seg_z = pl.BlockSpec((seg, w), lambda i, z: (z[0], 0))
        dw_out = call(
            k_dw_out, "dw_out", (1,), [seg_z] * 8 + [const((seg, D))] * 2, const((tp, w, D)),
            sds((tp, w, D), bf16), flops=2 * 2 * seg * D * D, nbytes=5 << 20,
        )(z, *ctxs[0], *ctxs[1], two[0][1], two[1][1])
        piece = dp_scatter(dw_out, dp, axis=1)
        own = piece[0].astype(f32)
        for r in range(1, tp):
            own = own + across(piece[r], r, tp).astype(f32)
        (g_out_w,) = placed(dp_gather(own.astype(bf16), dp), dp, f32)

        dw_qkv = call(
            k_dw_qkv, "dw_qkv", (D // tile,),
            [pl.BlockSpec((tokens, tile), lambda i, z: (0, i))] + [const((tokens, w))] * 3,
            rows_of((tile, 3 * w)), sds((D, 3 * w), bf16), flops=2 * tokens * D * 3 * w, nbytes=5 << 20,
        )(z, n_one, gq, gk, gv)
        g_q, g_k, g_v = placed(dp_gather(dp_scatter(dw_qkv, dp), dp), dp, f32, outs=3)

        mine = lax.dynamic_slice_in_dim(mix, zi * w, w, 1)
        up_sum = ffn[0][13] + ffn[1][13]
        vec = jnp.concatenate([
            mine[2], mine[3], mine[4], mine[5], mine[6], sums_qkv[0], sums_qkv[1],
            up_sum[1, :w], up_sum[0],
        ]).reshape(-1, 128)
        vec = dp_sum_small(vec, dp).reshape(-1)
        pieces = [vec[j * w:(j + 1) * w] for j in range(8)]
        g_up_b = vec[8 * w:]
        return (outputs, grad_inputs, pieces[0], pieces[1], g_q, pieces[5], g_k, g_v, pieces[6],
                g_out_w, pieces[4], pieces[2], pieces[3], g_up, g_up_b, g_down, pieces[7])

    return shards


def solution(mesh):
    return jax.shard_map(
        make_shards(mesh.shape["dp"], mesh.shape["tensor"]),
        mesh=mesh,
        in_specs=(
            P("dp", "tensor"), P("dp"), P("dp", "tensor", None, None), P("tensor"), P("tensor"),
            P(None, "tensor"), P("tensor"), P(None, "tensor"), P(None, "tensor"), P("tensor"),
            P("tensor", None), P("tensor"), P("tensor"), P("tensor"), P(None, "tensor"),
            P("tensor"), P("tensor", None), P("tensor"), P("dp", "tensor"),
        ),
        out_specs=(
            P("dp", "tensor"), P("dp", "tensor"), P("tensor"), P("tensor"), P(None, "tensor"),
            P("tensor"), P(None, "tensor"), P(None, "tensor"), P("tensor"), P("tensor", None),
            P("tensor"), P("tensor"), P("tensor"), P(None, "tensor"), P("tensor"),
            P("tensor", None), P("tensor"),
        ),
        check_vma=False,
    )
```

time: 724 us -> 447 us (0.62)
  waiting for transfers between devices: 458 us -> 185 us
  Pallas kernels: 0 us -> 123 us
  starting transfers between devices: 0.96 us -> 75.7 us
  matrix products: 83.1 us -> 11.9 us
  blocking collectives: 59.9 us -> 0 us
  local copies, waits for them, and re-layouts: 51.5 us -> 20.8 us
  other arithmetic: 36.4 us -> 22.7 us
  between operations: 15.2 us -> 2.32 us
  loops' own time: 9.58 us -> 0 us
    psum x2 -> x0, waiting for transfers between devices: 292 us -> none  [the longest x1 152 us: shards(): attn_full = lax.psum(attn_part, 'tensor')]
    ppermute x0 -> x66, waiting for transfers between devices: none -> 185 us  [the longest x35 122 us: across(): return lax.ppermute(value, 'tensor', [(i, i ^ mask) for i in range(size)])]
    pallas_call x0 -> x16, Pallas kernels: none -> 123 us  [the longest x2 27.6 us: shards(): call(partial(k_ffn, base), 'ffn', (steps,), [tw] * 4 + [hw] * 4 + [hd, co...]
    all_gather x3 -> x0, waiting for transfers between devices: 103 us -> none  [the longest x1 38 us: shards(): lax.all_gather(grad_resid_local.astype(bf16), 'tensor', axis=1, tiled=True)]
    ppermute x0 -> x66, starting transfers between devices: none -> 75.7 us  [the longest x35 50.3 us: across(): return lax.ppermute(value, 'tensor', [(i, i ^ mask) for i in range(size)])]
    dot_general x32 -> x2, matrix products: 83.1 us -> 11.9 us  [mm(): return lax.dot_general(left, right, dims, preferred_element_type=f32)]
    reduce_scatter x3 -> x0, waiting for transfers between devices: 62.2 us -> none  [the longest x1 42.2 us: shards(): lax.psum_scatter(grad_normed_two.astype(jnp.bfloat16), 'tensor', scatter_...]
    psum x3 -> x0, blocking collectives: 45.1 us -> none  [the longest x1 24.7 us: shards(): lax.psum((grad_attn_norm_gain, grad_attn_norm_bias, grad_query_weight, gr...]
  transfers between devices with their start and end apart: 8 -> 66, of which waited for: 7 -> 34; matrix products, arithmetic and copies ran while one was open for 12% -> 10% of each run, Pallas kernels for 0% -> 23%
where the time goes in v1:
time: 447 us; the launch traced here: 441 us
  waiting for transfers between devices  185 us (41%)
  Pallas kernels  123 us (28%)
  starting transfers between devices  75.7 us (17%)
  other arithmetic  22.7 us (5%)
  local copies, waits for them, and re-layouts  20.8 us (5%)
  matrix products  11.9 us (3%)
    ppermute x35, waiting for transfers between devices, across(): return lax.ppermute(value, 'tensor', [(i, i ^ mask) for i in range(size)])  122 us
    ppermute x31, waiting for transfers between devices, swap(): return lax.ppermute(value, 'dp', [(i, i ^ mask) for i in range(size)])  62.1 us
    ppermute x35, starting transfers between devices, across(): return lax.ppermute(value, 'tensor', [(i, i ^ mask) for i in range(size)])  50.3 us
    pallas_call x2, Pallas kernels, shards(): call(partial(k_ffn, base), 'ffn', (steps,), [tw] * 4 + [hw] * 4 + [hd, co...  27.6 us
    ppermute x31, starting transfers between devices, swap(): return lax.ppermute(value, 'dp', [(i, i ^ mask) for i in range(size)])  25.5 us
    pallas_call x1, Pallas kernels, shards(): call(k_attend_back, 'attend_back', (heads // 2,), [pair, pair, pair, prob...  21.7 us
    pallas_call x3, Pallas kernels, placed(): call(k_place, 'place', (n,), [pl.BlockSpec((1,) + tuple(value.shape[1:]),...  16.1 us
    pallas_call x2, Pallas kernels, shards(): call(k_attend, 'attend', (steps,), [pl.BlockSpec((tile, w), lambda i, z,...  15.9 us
  transfers between devices with their start and end apart: 66, of which 34 were waited for; matrix products, arithmetic and copies ran while one was open for 10% of the time, Pallas kernels for 23%

profile of v1, /device:TPU:0, one launch (start us, length us, event | category | flops | bytes accessed | tf_op | source)
XLA Modules:
  0.0 441.5 jit_solution(13380176157821766362)
XLA Ops:
  15.3 24.1 %collective-permute-done.1.x2.s2 = bf16[1168,256]{1,0:T(8,128)(2,1)S(1)} collective-permute-done((bf16[1168,256]{1,0:T(8,128)(2,1)S(1)}, bf16[1168,256]{1,0:T(8,128)(2,1)S(1)}, u32[]{:S(2)}, u32[]{:S(2)}) %collective-permute-start.1) | collective-permute-done | bytes 598048 | tf_op jit(solution)/shard_map/ppermute | solution.py:66
  42.1 11.9 %collective-permute-done.2.x3.s3 = bf16[1168,256]{1,0:T(8,128)(2,1)S(1)} collective-permute-done((bf16[1168,256]{1,0:T(8,128)(2,1)S(1)}, bf16[1168,256]{1,0:T(8,128)(2,1)S(1)}, u32[]{:S(2)}, u32[]{:S(2)}) %collective-permute-start.2) | collective-permute-done | bytes 598048 | tf_op jit(solution)/shard_map/ppermute | solution.py:66
  54.8 6.8 %qkv.1 = (bf16[1024,1024]{1,0:T(8,128)(2,1)}, bf16[1024,1024]{1,0:T(8,128)(2,1)}, bf16[1024,256]{1,0:T(8,128)(2,1)}, bf16[1024,256]{1,0:T(8,128)(2,1)}, bf16[102...) custom-call(s32[1]{0:T(128)} %bitcast.z_ref, bf16[1168,256]{1,0:T(8,128)(2,1)} %copy-done.4, ...), custom_call_target="tpu_custom_call" | custom-call | tf_op jit(solution)/shard_map/qkv/pallas_call | solution.py:469
  61.6 7.9 %attend.2 = (bf16[512,256]{1,0:T(8,128)(2,1)}, bf16[4,512,1024]{2,1,0:T(8,128)(2,1)}) custom-call(s32[1]{0:T(128)} %bitcast.z_ref, bf16[1024,256]{1,0:T(8,128)(2,1)} %get-tuple-element.91.q, bf16[1024,256]{1,0:T(8,128)(2,1)} %get-tuple-element.92.k, bf16[1024,256]{1,0:T(8,128)(2,1)} %get-tuple-element.93.v, f32[64,1024]{1,0:T(8,128)} %and_select_fusion.bias), custom_call_target="tpu_custom_call" | custom-call | tf_op jit(solution)/shard_map/attend/pallas_call | solution.py:487
  81.2 7.9 %attend.3 = (bf16[512,256]{1,0:T(8,128)(2,1)}, bf16[4,512,1024]{2,1,0:T(8,128)(2,1)}) custom-call(s32[1]{0:T(128)} %bitcast.z_ref, bf16[1024,256]{1,0:T(8,128)(2,1)} %get-tuple-element.91.q, bf16[1024,256]{1,0:T(8,128)(2,1)} %get-tuple-element.92.k, bf16[1024,256]{1,0:T(8,128)(2,1)} %get-tuple-element.93.v, f32[64,1024]{1,0:T(8,128)} %and_select_fusion.bias), custom_call_target="tpu_custom_call" | custom-call | tf_op jit(solution)/shard_map/attend/pallas_call | solution.py:487
  95.3 9.5 %collective-permute-done.7.g2 = bf16[1024,256]{1,0:T(8,128)(2,1)S(1)} collective-permute-done((bf16[1024,256]{1,0:T(8,128)(2,1)S(1)}, bf16[1024,256]{1,0:T(8,128)(2,1)S(1)}, u32[]{:S(2)}, u32[]{:S(2)}) %collective-permute-start.7) | collective-permute-done | bytes 524320 | tf_op jit(solution)/shard_map/ppermute | solution.py:66
  114.2 19.7 %collective-permute-done.4.c2.b2 = bf16[512,256]{1,0:T(8,128)(2,1)S(1)} collective-permute-done((bf16[512,256]{1,0:T(8,128)(2,1)S(1)}, bf16[512,256]{1,0:T(8,128)(2,1)S(1)}, u32[]{:S(2)}, u32[]{:S(2)}) %collective-permute-start.4) | collective-permute-done | bytes 262176 | tf_op jit(solution)/shard_map/ppermute | solution.py:66
  138.3 5.5 %place.3.wo = bf16[3,256,1024]{2,1,0:T(8,128)(2,1)} custom-call(s32[1]{0:T(128)} %bitcast.5.p_ref, bf16[8,3,32,1024]{3,2,1,0:T(8,128)(2,1)} %bitcast.109), custom_call_target="tpu_custom_call" | custom-call | tf_op jit(solution)/shard_map/place/pallas_call | solution.py:164
  145.3 13.7 %ffn.2 = (bf16[1024,1024]{1,0:T(8,128)(2,1)}, f32[1024,1024]{1,0:T(8,128)}, bf16[1024,1024]{1,0:T(8,128)(2,1)}, bf16[1024,1024]{1,0:T(8,128)(2,1)}, bf16[1024,10...) custom-call(s32[1]{0:T(128)} %bitcast.z_ref, ...), custom_call_target="tpu_custom_call" | custom-call | tf_op jit(solution)/shard_map/ffn/pallas_call | solution.py:510
  162.0 13.9 %ffn.3 = (bf16[1024,1024]{1,0:T(8,128)(2,1)}, f32[1024,1024]{1,0:T(8,128)}, bf16[1024,1024]{1,0:T(8,128)(2,1)}, bf16[1024,1024]{1,0:T(8,128)(2,1)}, bf16[1024,10...) custom-call(s32[1]{0:T(128)} %bitcast.z_ref, ...), custom_call_target="tpu_custom_call", output_to_operand_aliasing={{0}: (16, {}), {1}: (17, {}), {2}: (18, {}), {3}: (19, {}),... | custom-call | tf_op jit(solution)/shard_map/ffn/pallas_call | solution.py:510
  181.0 6.0 %convolution_convert_fusion.1 = bf16[1024,1024]{1,0:T(8,128)(2,1)} fusion(bf16[1024,1024]{1,0:T(8,128)(2,1)} %get-tuple-element.160, bf16[1024,1024]{1,0:T(8,128)(2,1)} %get-tuple-element.161), kind=kOutput, calls=%fused_computation.5 | convolution fusion | flops 2148532224 | bytes 6291456 | tf_op jit(solution)/shard_map/dot_general | solution.py:25
  204.4 6.0 %broadcast_select_fusion = (bf16[1024,1024]{1,0:T(8,128)(2,1)}, bf16[1024,1024]{1,0:T(8,128)(2,1)}) fusion(bf16[1024,1024]{1,0:T(8,128)(2,1)} %convolution_convert_fusion.1, pred[]{:T(512)S(6)} %eq.53, bf16[1024,1024]{1,0:T(8,128)(2,1)} %get-tuple-element.162, bf16[1024,1024]{1,0:T(8,128)(2,1)S(1)} %copy-done), kind=kOutput, calls=%fused_computation.3 | convolution fusion | flops 2149580800 | bytes 10485761 | tf_op jit(solution)/shard_map/dot_general | solution.py:25
  226.7 21.7 %attend_back.1 = (bf16[1024,256]{1,0:T(8,128)(2,1)}, bf16[1024,256]{1,0:T(8,128)(2,1)}, bf16[1024,256]{1,0:T(8,128)(2,1)}, f32[8,256]{1,0:T(8,128)}) custom-call(s32[1]{0:T(128)} %bitcast.z_ref, bf16[1024,256]{1,0:T(8,128)(2,1)} %get-tuple-element.91.q, bf16[1024,256]{1,0:T(8,128)(2,1)} %get-tuple-element.92.k, bf16[1024,256]{1,0:T(8,128)(2,1)} %get-tuple-element.93.v, ...), custom_call_target="tpu_custom_call" | custom-call | tf_op jit(solution)/shard_map/attend_back/pallas_call | solution.py:549
  248.4 5.4 %dw_qkv.1 = bf16[1024,768]{1,0:T(8,128)(2,1)} custom-call(s32[1]{0:T(128)} %bitcast.z_ref, bf16[1024,1024]{1,0:T(8,128)(2,1)} %get-tuple-element.154.n, bf16[1024,256]{1,0:T(8,128)(2,1)} %get-tuple-element.136.gq, bf16[1024,256]{1,0:T(8,128)(2,1)} %get-tuple-element.137.gk, bf16[1024,256]{1,0:T(8,128)(2,1)} %get-tuple-element.138.gv), custom_call_target="tpu_custom_call" | custom-call | tf_op jit(solution)/shard_map/dw_qkv/pallas_call | solution.py:594
  253.8 7.7 %norm_one.1 = (bf16[1024,256]{1,0:T(8,128)(2,1)}, bf16[1024,256]{1,0:T(8,128)(2,1)}, bf16[1024,256]{1,0:T(8,128)(2,1)}, bf16[1024,256]{1,0:T(8,128)(2,1)}, f32[8,1024]{1,0:T(8,128)}, /*index=5*/f32[8,1024]{1,0:T(8,128)}) custom-call(s32[1]{0:T(128)} %bitcast.z_ref, bf16[1024,256]{1,0:T(8,128)(2,1)} %get-tuple-element.136.gq, ...), custom_call_target="tpu_custom_call" | custom-call | tf_op jit(solution)/shard_map/norm_one/pallas_call | solution.py:560
  290.3 9.4 %collective-permute-done.59 = bf16[256,1024]{1,0:T(8,128)(2,1)S(1)} collective-permute-done((bf16[256,1024]{1,0:T(8,128)(2,1)S(1)}, bf16[256,1024]{1,0:T(8,128)(2,1)S(1)}, u32[]{:S(2)}, u32[]{:S(2)}) %collective-permute-start.59) | collective-permute-done | bytes 524320 | tf_op jit(solution)/shard_map/ppermute | solution.py:70
  300.2 10.2 %collective-permute-done.60 = bf16[256,1024]{1,0:T(8,128)(2,1)S(1)} collective-permute-done((bf16[256,1024]{1,0:T(8,128)(2,1)S(1)}, bf16[256,1024]{1,0:T(8,128)(2,1)S(1)}, u32[]{:S(2)}, u32[]{:S(2)}) %collective-permute-start.60) | collective-permute-done | bytes 524320 | tf_op jit(solution)/shard_map/ppermute | solution.py:70
  333.4 8.6 %collective-permute-done.62 = bf16[1,256,1024]{2,1,0:T(8,128)(2,1)} collective-permute-done((bf16[1,256,1024]{2,1,0:T(8,128)(2,1)S(1)}, bf16[1,256,1024]{2,1,0:T(8,128)(2,1)}, u32[]{:S(2)}, u32[]{:S(2)}) %collective-permute-start.62) | collective-permute-done | bytes 524320 | tf_op jit(solution)/shard_map/ppermute | solution.py:70
  342.5 7.9 %collective-permute-done.63 = bf16[1,256,1024]{2,1,0:T(8,128)(2,1)} collective-permute-done((bf16[1,256,1024]{2,1,0:T(8,128)(2,1)S(1)}, bf16[1,256,1024]{2,1,0:T(8,128)(2,1)}, u32[]{:S(2)}, u32[]{:S(2)}) %collective-permute-start.63) | collective-permute-done | bytes 524320 | tf_op jit(solution)/shard_map/ppermute | solution.py:70
  355.7 8.4 %collective-permute-done.23 = bf16[1024,256]{1,0:T(8,128)(2,1)S(1)} collective-permute-done((bf16[1024,256]{1,0:T(8,128)(2,1)S(1)}, bf16[1024,256]{1,0:T(8,128)(2,1)S(1)}, u32[]{:S(2)}, u32[]{:S(2)}) %collective-permute-start.23) | collective-permute-done | bytes 524320 | tf_op jit(solution)/shard_map/ppermute | solution.py:66
  370.2 16.7 %collective-permute-done.52 = bf16[32,1024]{1,0:T(8,128)(2,1)S(1)} collective-permute-done((bf16[32,1024]{1,0:T(8,128)(2,1)S(1)}, bf16[32,1024]{1,0:T(8,128)(2,1)S(1)}, u32[]{:S(2)}, u32[]{:S(2)}) %collective-permute-start.52) | collective-permute-done | bytes 65568 | tf_op jit(solution)/shard_map/ppermute | solution.py:66
  411.3 7.4 %collective-permute-done.24 = bf16[1024,256]{1,0:T(8,128)(2,1)} collective-permute-done((bf16[1024,256]{1,0:T(8,128)(2,1)}, bf16[1024,256]{1,0:T(8,128)(2,1)}, u32[]{:S(2)}, u32[]{:S(2)}) %collective-permute-start.24) | collective-permute-done | bytes 524320 | tf_op jit(solution)/shard_map/ppermute | solution.py:66
  429.0 5.7 %place.4 = (f32[1024,256]{1,0:T(8,128)}, f32[1024,256]{1,0:T(8,128)}, f32[1024,256]{1,0:T(8,128)}) custom-call(s32[1]{0:T(128)} %bitcast.5.p_ref, bf16[8,128,768]{2,1,0:T(8,128)(2,1)} %bitcast.108), custom_call_target="tpu_custom_call" | custom-call | tf_op jit(solution)/shard_map/place/pallas_call | solution.py:164
  434.8 6.6 %place_two.1 = (f32[1024,1024]{1,0:T(8,128)}, f32[1024,1024]{1,0:T(8,128)}) custom-call(s32[2]{0:T(128)} %pad_add_fusion.p_ref, bf16[4,256,1024]{2,1,0:T(8,128)(2,1)} %copy-done.2, bf16[4,256,1024]{2,1,0:T(8,128)(2,1)} %collective-permute-done.65.two), custom_call_target="tpu_custom_call" | custom-call | tf_op jit(solution)/shard_map/place_two/pallas_call | solution.py:196
  (302 shorter events, 190.6 us)
Async XLA Ops:
  8.8 30.5 %collective-permute-start.1 = (bf16[1168,256]{1,0:T(8,128)(2,1)S(1)}, bf16[1168,256]{1,0:T(8,128)(2,1)S(1)}, u32[]{:S(2)}, u32[]{:S(2)}) collective-permute-start(bf16[1168,256]{1,0:T(8,128)(2,1)S(1)} %concatenate.13.x0.s0), channel_id=1, source_target_pairs={{0,2},{1,3},{2,0},{3,1},{4,6},{5,7},{6,4},{7,5},{8,10},{9,11},{10,... | collective-permute-start | bytes 1794056 | tf_op jit(solution)/shard_map/ppermute | solution.py:66
  12.9 29.1 %collective-permute-start = (bf16[1168,256]{1,0:T(8,128)(2,1)S(1)}, bf16[1168,256]{1,0:T(8,128)(2,1)S(1)}, u32[]{:S(2)}, u32[]{:S(2)}) collective-permute-start(bf16[1168,256]{1,0:T(8,128)(2,1)S(1)} %concatenate.13.x0.s0), channel_id=1, source_target_pairs={{0,1},{1,0},{2,3},{3,2},{4,5},{5,4},{6,7},{7,6},{8,9},{9,8},{10,11... | collective-permute-start | bytes 1794056 | tf_op jit(solution)/shard_map/ppermute | solution.py:66
  73.1 31.8 %collective-permute-start.7 = (bf16[1024,256]{1,0:T(8,128)(2,1)S(1)}, bf16[1024,256]{1,0:T(8,128)(2,1)S(1)}, u32[]{:S(2)}, u32[]{:S(2)}) collective-permute-start(bf16[1024,256]{1,0:T(8,128)(2,1)S(1)} %copy-done.10), channel_id=1, source_target_pairs={{0,2},{1,3},{2,0},{3,1},{4,6},{5,7},{6,4},{7,5},{8,10},{9,11},{10,... | collective-permute-start | bytes 1572872 | tf_op jit(solution)/shard_map/ppermute | solution.py:66
  81.2 54.6 %collective-permute-start.12 = (bf16[4,3,32,1024]{3,2,1,0:T(8,128)(2,1)}, bf16[4,3,32,1024]{3,2,1,0:T(8,128)(2,1)}, u32[]{:S(2)}, u32[]{:S(2)}) collective-permute-start(bf16[4,3,32,1024]{3,2,1,0:T(8,128)(2,1)} %get-tuple-element.177), channel_id=1, source_target_pairs={{0,4},{4,0},{8,12},{12,8},{16,20},{20,16},{24,28},{28,24},{1,5},{5... | collective-permute-start | bytes 2359304 | tf_op jit(solution)/shard_map/ppermute | solution.py:70
  94.7 49.6 %collective-permute-start.6 = (bf16[1024,256]{1,0:T(8,128)(2,1)S(1)}, bf16[1024,256]{1,0:T(8,128)(2,1)S(1)}, u32[]{:S(2)}, u32[]{:S(2)}) collective-permute-start(bf16[1024,256]{1,0:T(8,128)(2,1)S(1)} %copy-done.10), channel_id=1, source_target_pairs={{0,1},{1,0},{2,3},{3,2},{4,5},{5,4},{6,7},{7,6},{8,9},{9,8},{10,11... | collective-permute-start | bytes 1572872 | tf_op jit(solution)/shard_map/ppermute | solution.py:66
  104.8 39.5 %collective-permute-start.8 = (bf16[1024,256]{1,0:T(8,128)(2,1)S(1)}, bf16[1024,256]{1,0:T(8,128)(2,1)S(1)}, u32[]{:S(2)}, u32[]{:S(2)}) collective-permute-start(bf16[1024,256]{1,0:T(8,128)(2,1)S(1)} %collective-permute-done.7.g2), channel_id=1, source_target_pairs={{0,1},{1,0},{2,3},{3,2},{4,5},{5,4},{6,7},{7,6},{8,9},{9,8},{10,11... | collective-permute-start | bytes 1572872 | tf_op jit(solution)/shard_map/ppermute | solution.py:66
  109.5 24.3 %collective-permute-start.4 = (bf16[512,256]{1,0:T(8,128)(2,1)S(1)}, bf16[512,256]{1,0:T(8,128)(2,1)S(1)}, u32[]{:S(2)}, u32[]{:S(2)}) collective-permute-start(bf16[512,256]{1,0:T(8,128)(2,1)S(1)} %copy-done.9), channel_id=1, source_target_pairs={{0,2},{1,3},{2,0},{3,1},{4,6},{5,7},{6,4},{7,5},{8,10},{9,11},{10,... | collective-permute-start | bytes 786440 | tf_op jit(solution)/shard_map/ppermute | solution.py:66
  110.6 33.7 %collective-permute-start.15 = (bf16[512,256]{1,0:T(8,128)(2,1)}, bf16[512,256]{1,0:T(8,128)(2,1)}, u32[]{:S(2)}, u32[]{:S(2)}) collective-permute-start(bf16[512,256]{1,0:T(8,128)(2,1)} %collective-permute-done.14.c2.a2), channel_id=1, source_target_pairs={{0,1},{1,0},{2,3},{3,2},{4,5},{5,4},{6,7},{7,6},{8,9},{9,8},{10,11... | collective-permute-start | bytes 786440 | tf_op jit(solution)/shard_map/ppermute | solution.py:66
  133.9 27.3 %collective-permute-start.3 = (bf16[512,256]{1,0:T(8,128)(2,1)S(1)}, bf16[512,256]{1,0:T(8,128)(2,1)S(1)}, u32[]{:S(2)}, u32[]{:S(2)}) collective-permute-start(bf16[512,256]{1,0:T(8,128)(2,1)S(1)} %copy-done.9), channel_id=1, source_target_pairs={{0,1},{1,0},{2,3},{3,2},{4,5},{5,4},{6,7},{7,6},{8,9},{9,8},{10,11... | collective-permute-start | bytes 786440 | tf_op jit(solution)/shard_map/ppermute | solution.py:66
  135.8 25.4 %collective-permute-start.5 = (bf16[512,256]{1,0:T(8,128)(2,1)S(1)}, bf16[512,256]{1,0:T(8,128)(2,1)S(1)}, u32[]{:S(2)}, u32[]{:S(2)}) collective-permute-start(bf16[512,256]{1,0:T(8,128)(2,1)S(1)} %collective-permute-done.4.c2.b2), channel_id=1, source_target_pairs={{0,1},{1,0},{2,3},{3,2},{4,5},{5,4},{6,7},{7,6},{8,9},{9,8},{10,11... | collective-permute-start | bytes 786440 | tf_op jit(solution)/shard_map/ppermute | solution.py:66
  160.6 31.6 %collective-permute-start.25 = (bf16[128,1024]{1,0:T(8,128)(2,1)}, bf16[128,1024]{1,0:T(8,128)(2,1)S(1)}, u32[]{:S(2)}, u32[]{:S(2)}) collective-permute-start(bf16[128,1024]{1,0:T(8,128)(2,1)} %get-tuple-element.129), channel_id=1, source_target_pairs={{0,1},{1,0},{2,3},{3,2},{4,5},{5,4},{6,7},{7,6},{8,9},{9,8},{10,11... | collective-permute-start | bytes 786440 | tf_op jit(solution)/shard_map/ppermute | solution.py:66
  177.4 35.5 %collective-permute-start.16 = (bf16[128,1024]{1,0:T(8,128)(2,1)}, bf16[128,1024]{1,0:T(8,128)(2,1)S(1)}, u32[]{:S(2)}, u32[]{:S(2)}) collective-permute-start(bf16[128,1024]{1,0:T(8,128)(2,1)} %get-tuple-element.114), channel_id=1, source_target_pairs={{0,1},{1,0},{2,3},{3,2},{4,5},{5,4},{6,7},{7,6},{8,9},{9,8},{10,11... | collective-permute-start | bytes 786440 | tf_op jit(solution)/shard_map/ppermute | solution.py:66
  222.8 58.7 %collective-permute-start.58 = (bf16[1024,1024]{1,0:T(8,128)(2,1)}, bf16[1024,1024]{1,0:T(8,128)(2,1)}, u32[]{:S(2)}, u32[]{:S(2)}) collective-permute-start(bf16[1024,1024]{1,0:T(8,128)(2,1)} %get-tuple-element.198), channel_id=1, source_target_pairs={{0,4},{4,0},{8,12},{12,8},{16,20},{20,16},{24,28},{28,24},{1,5},{5... | collective-permute-start | bytes 6291464 | tf_op jit(solution)/shard_map/ppermute | solution.py:70
  279.8 32.8 %collective-permute-start.38 = (f32[24,128]{1,0:T(8,128)S(1)}, f32[24,128]{1,0:T(8,128)S(1)}, u32[]{:S(2)}, u32[]{:S(2)}) collective-permute-start(f32[24,128]{1,0:T(8,128)S(1)} %fusion.18), channel_id=1, source_target_pairs={{0,16},{4,20},{8,24},{12,28},{16,0},{20,4},{24,8},{28,12},{1,17},{... | collective-permute-start | bytes 36872 | tf_op jit(solution)/shard_map/ppermute | solution.py:70
  285.4 25.0 %collective-permute-start.60 = (bf16[256,1024]{1,0:T(8,128)(2,1)S(1)}, bf16[256,1024]{1,0:T(8,128)(2,1)S(1)}, u32[]{:S(2)}, u32[]{:S(2)}) collective-permute-start(bf16[256,1024]{1,0:T(8,128)(2,1)S(1)} %get-tuple-element.167), channel_id=1, source_target_pairs={{0,16},{4,20},{8,24},{12,28},{16,0},{20,4},{24,8},{28,12},{1,17},{... | collective-permute-start | bytes 1572872 | tf_op jit(solution)/shard_map/ppermute | solution.py:70
  286.6 24.4 %collective-permute-start.61 = (bf16[256,1024]{1,0:T(8,128)(2,1)S(1)}, bf16[256,1024]{1,0:T(8,128)(2,1)S(1)}, u32[]{:S(2)}, u32[]{:S(2)}) collective-permute-start(bf16[256,1024]{1,0:T(8,128)(2,1)S(1)} %get-tuple-element.166), channel_id=1, source_target_pairs={{0,24},{4,28},{8,16},{12,20},{16,8},{20,12},{24,0},{28,4},{1,25},{... | collective-permute-start | bytes 1572872 | tf_op jit(solution)/shard_map/ppermute | solution.py:70
  288.4 26.8 %collective-permute-start.40 = (bf16[128,768]{1,0:T(8,128)(2,1)S(1)}, bf16[128,768]{1,0:T(8,128)(2,1)S(1)}, u32[]{:S(2)}, u32[]{:S(2)}) collective-permute-start(bf16[128,768]{1,0:T(8,128)(2,1)S(1)} %get-tuple-element.173), channel_id=1, source_target_pairs={{0,8},{4,12},{8,0},{12,4},{16,24},{20,28},{24,16},{28,20},{1,9},{5... | collective-permute-start | bytes 589832 | tf_op jit(solution)/shard_map/ppermute | solution.py:70
  319.8 30.6 %collective-permute-start.63 = (bf16[1,256,1024]{2,1,0:T(8,128)(2,1)S(1)}, bf16[1,256,1024]{2,1,0:T(8,128)(2,1)}, u32[]{:S(2)}, u32[]{:S(2)}) collective-permute-start(bf16[1,256,1024]{2,1,0:T(8,128)(2,1)S(1)} %bitcast.112), channel_id=1, source_target_pairs={{0,16},{4,20},{8,24},{12,28},{16,0},{20,4},{24,8},{28,12},{1,17},{... | collective-permute-start | bytes 1572872 | tf_op jit(solution)/shard_map/ppermute | solution.py:70
  325.0 28.2 %collective-permute-start.64 = (bf16[1,256,1024]{2,1,0:T(8,128)(2,1)S(1)}, bf16[1,256,1024]{2,1,0:T(8,128)(2,1)}, u32[]{:S(2)}, u32[]{:S(2)}) collective-permute-start(bf16[1,256,1024]{2,1,0:T(8,128)(2,1)S(1)} %bitcast.113), channel_id=1, source_target_pairs={{0,24},{4,28},{8,16},{12,20},{16,8},{20,12},{24,0},{28,4},{1,25},{... | collective-permute-start | bytes 1572872 | tf_op jit(solution)/shard_map/ppermute | solution.py:70
  330.2 24.9 %collective-permute-start.32 = (bf16[1024,256]{1,0:T(8,128)(2,1)}, bf16[1024,256]{1,0:T(8,128)(2,1)S(1)}, u32[]{:S(2)}, u32[]{:S(2)}) collective-permute-start(bf16[1024,256]{1,0:T(8,128)(2,1)} %get-tuple-element.144), channel_id=1, source_target_pairs={{0,1},{1,0},{2,3},{3,2},{4,5},{5,4},{6,7},{7,6},{8,9},{9,8},{10,11... | collective-permute-start | bytes 1572872 | tf_op jit(solution)/shard_map/ppermute | solution.py:66
  330.7 66.8 %collective-permute-start.31 = (bf16[1024,256]{1,0:T(8,128)(2,1)}, bf16[1024,256]{1,0:T(8,128)(2,1)S(1)}, u32[]{:S(2)}, u32[]{:S(2)}) collective-permute-start(bf16[1024,256]{1,0:T(8,128)(2,1)} %get-tuple-element.142), channel_id=1, source_target_pairs={{0,1},{1,0},{2,3},{3,2},{4,5},{5,4},{6,7},{7,6},{8,9},{9,8},{10,11... | collective-permute-start | bytes 1572872 | tf_op jit(solution)/shard_map/ppermute | solution.py:66
  355.0 79.8 %collective-permute-start.65 = (bf16[4,256,1024]{2,1,0:T(8,128)(2,1)S(1)}, bf16[4,256,1024]{2,1,0:T(8,128)(2,1)}, u32[]{:S(2)}, u32[]{:S(2)}) collective-permute-start(bf16[4,256,1024]{2,1,0:T(8,128)(2,1)S(1)} %maximum_bitcast_fusion.one), channel_id=1, source_target_pairs={{0,4},{4,0},{8,12},{12,8},{16,20},{20,16},{24,28},{28,24},{1,5},{5... | collective-permute-start | bytes 6291464 | tf_op jit(solution)/shard_map/ppermute | solution.py:70
  364.1 33.9 %collective-permute-start.33 = (bf16[1024,256]{1,0:T(8,128)(2,1)S(1)}, bf16[1024,256]{1,0:T(8,128)(2,1)S(1)}, u32[]{:S(2)}, u32[]{:S(2)}) collective-permute-start(bf16[1024,256]{1,0:T(8,128)(2,1)S(1)} %add_convert_fusion.4), channel_id=1, source_target_pairs={{0,2},{1,3},{2,0},{3,1},{4,6},{5,7},{6,4},{7,5},{8,10},{9,11},{10,... | collective-permute-start | bytes 1572872 | tf_op jit(solution)/shard_map/ppermute | solution.py:66
  398.0 28.6 %collective-permute-start.46 = (bf16[4,128,768]{2,1,0:T(8,128)(2,1)}, bf16[4,128,768]{2,1,0:T(8,128)(2,1)}, u32[]{:S(2)}, u32[]{:S(2)}) collective-permute-start(bf16[4,128,768]{2,1,0:T(8,128)(2,1)} %get-tuple-element.172), channel_id=1, source_target_pairs={{0,4},{4,0},{8,12},{12,8},{16,20},{20,16},{24,28},{28,24},{1,5},{5... | collective-permute-start | bytes 2359304 | tf_op jit(solution)/shard_map/ppermute | solution.py:70
  (88 other events, 1010.3 us)
